TPU v7x, 32 devices: a whole 2x2x4 slice. The times are simulated.
32 devices in a mesh: dp: 16 (over z, y, core), slab: 2 (over x).
Axes of the slice: x: 2, y: 2, z: 4, core: 2. Of those that a mesh axis runs over, the one named last changes fastest.
Arguments:
- snapshots: bfloat16 [16, 64, 512, 512], P('dp', None, 'slab'), may hold values from -6 to 6
- cotangent: bfloat16 [16, 64, 512, 512], P('dp', None, 'slab'), may hold values from -6 to 6
- w_spec: float32 [32, 32, 64, 128], P('slab', 'dp'), may hold values from -0.5 to 0.5
- first_moment: float32 [32, 32, 64, 128], P('slab', 'dp'), may hold values from -6 to 6
- second_moment: float32 [32, 32, 64, 128], P('slab', 'dp'), may hold values from 0.1 to 4
- w_skip: bfloat16 [64, 64], replicated, may hold values from -0.75 to 0.75
- bias: float32 [64], replicated, may hold values from -3 to 3
Outputs:
- layer_out: bfloat16 [16, 64, 512, 512], P('dp', None, 'slab')
- new_weights: float32 [32, 32, 64, 128], P('slab', 'dp')
- new_first: float32 [32, 32, 64, 128], P('slab', 'dp')
- new_second: float32 [32, 32, 64, 128], P('slab', 'dp')
All inputs are finite; a program needn't handle non-finite values.
Results may differ from a plain program's by a relative error of at most 0.001.
Values sent between devices are 32-bit elements; how exact they have to be, the bound alone decides.
A program may use at most 192 MiB of HBM per device.

v0:
```python
import math
import jax
import jax.numpy as jnp
from jax import lax
from jax.sharding import PartitionSpec as P

NY = 512
NZ = 512
KY = 32
KZ = 32
high = lax.Precision.HIGHEST
gelu_coef = 0.7978845608028654
cube_coef = 0.044715


def gelu_value(x):
    return 0.5 * x * (1.0 + jnp.tanh(gelu_coef * (x + cube_coef * x * x * x)))


def gelu_slope(x):
    tanh_val = jnp.tanh(gelu_coef * (x + cube_coef * x * x * x))
    return 0.5 * (1.0 + tanh_val) + 0.5 * x * (1.0 - tanh_val * tanh_val) * gelu_coef * (
        1.0 + 3.0 * cube_coef * x * x
    )


def z_tables(length):
    zpos = jnp.arange(length, dtype=jnp.int32)[:, None]
    kpos = jnp.arange(KZ, dtype=jnp.int32)[None, :]
    angle = 2.0 * math.pi / length * jnp.remainder(zpos * kpos, length).astype(jnp.float32)
    return (jnp.cos(angle), jnp.sin(angle))


def y_tables(count):
    half = KY // 2
    freq = jnp.concatenate(
        [jnp.arange(half, dtype=jnp.int32), jnp.arange(half, dtype=jnp.int32) - half]
    )
    ypos = jnp.arange(count, dtype=jnp.int32)
    phase = jnp.remainder(ypos[:, None] * freq[None, :], NY)
    angle = 2.0 * math.pi / NY * phase.astype(jnp.float32)
    return (jnp.cos(angle), jnp.sin(angle))


def y_forward(flat, ycos, ysin, count):
    with_cos = jnp.einsum("cyk,yj->ckj", flat, ycos, precision=high)
    with_sin = jnp.einsum("cyk,yj->ckj", flat, ysin, precision=high)
    real_part = with_cos[:, :count] + with_sin[:, count:]
    imag_part = with_cos[:, count:] - with_sin[:, :count]
    return jnp.stack([real_part, imag_part], 0).transpose(2, 0, 1, 3)


def y_inverse(spec, ycos, ysin):
    vreal = spec[:, 0]
    vimag = spec[:, 1]
    yreal = jnp.einsum("koj,yj->oyk", vreal, ycos, precision=high) - jnp.einsum(
        "koj,yj->oyk", vimag, ysin, precision=high
    )
    yimag = jnp.einsum("koj,yj->oyk", vreal, ysin, precision=high) + jnp.einsum(
        "koj,yj->oyk", vimag, ycos, precision=high
    )
    return (yreal, yimag)


def forward_modes(field):
    chans, rows, length = field.shape
    zcos, zsin = z_tables(length)
    table = jnp.concatenate([zcos, -zsin], axis=1)
    along_z = jnp.dot(
        field.reshape(chans * rows, length),
        table,
        precision=high,
        preferred_element_type=jnp.float32,
    )
    along_z = along_z.reshape(chans, rows, 2, KZ)
    pencil = lax.all_to_all(along_z, "slab", split_axis=3, concat_axis=1, tiled=True)
    local_modes = pencil.shape[3]
    ycos, ysin = y_tables(NY)
    return y_forward(pencil.reshape(chans, NY, 2 * local_modes), ycos, ysin, local_modes)


def inverse_modes(spec, rows, length):
    chans = spec.shape[2]
    zcos, zsin = z_tables(length)
    ycos, ysin = y_tables(NY)
    yreal, yimag = y_inverse(spec, ycos, ysin)
    both = jnp.stack([yreal, yimag], 2)
    slabs = lax.all_to_all(both, "slab", split_axis=1, concat_axis=3, tiled=True)
    back_table = jnp.concatenate([zcos.T, -zsin.T], axis=0)
    total = jnp.dot(
        slabs.reshape(chans * rows, 2 * KZ),
        back_table,
        precision=high,
        preferred_element_type=jnp.float32,
    )
    return total.reshape(chans, rows, length)


def body(snapshots, cotangent, w_spec, first_moment, second_moment, w_skip, bias):
    chans, rows, length = snapshots.shape[1:]
    spec_scale = 1.0 / math.sqrt(NY * NZ)
    out_scale = 1.0 / math.sqrt(KY * KZ)
    count = lax.axis_size("dp")
    field_low = snapshots[0]
    weights = lax.all_gather(w_spec, "dp", axis=1, tiled=True)
    spec_u = forward_modes(field_low.astype(jnp.float32)) * spec_scale
    ureal = spec_u[:, 0]
    uimag = spec_u[:, 1]
    first_part = jnp.einsum("kij,kjio->koj", ureal, weights, precision=high)
    second_part = jnp.einsum("kij,kjio->koj", uimag, weights, precision=high)
    vreal = first_part[:, :chans] - second_part[:, chans:]
    vimag = first_part[:, chans:] + second_part[:, :chans]
    spec_v = jnp.stack([vreal, vimag], 1)
    mixed = inverse_modes(spec_v, rows, length) * out_scale
    skip = jnp.einsum(
        "io,in->on",
        w_skip,
        field_low.reshape(chans, rows * length),
        preferred_element_type=jnp.float32,
    )
    pre = mixed + skip.reshape(chans, rows, length) + bias[:, None, None]
    layer_out = gelu_value(pre).astype(jnp.bfloat16)[None]
    slope = cotangent[0].astype(jnp.float32) * gelu_slope(pre)
    spec_g = forward_modes(slope) * out_scale
    greal = spec_g[:, 0]
    gimag = spec_g[:, 1]
    grad_real = jnp.einsum("kij,koj->kjio", ureal, greal, precision=high) + jnp.einsum(
        "kij,koj->kjio", uimag, gimag, precision=high
    )
    grad_imag = jnp.einsum("kij,koj->kjio", ureal, gimag, precision=high) - jnp.einsum(
        "kij,koj->kjio", uimag, greal, precision=high
    )
    summed = lax.psum_scatter(
        jnp.concatenate([grad_real, grad_imag], axis=-1), "dp", scatter_dimension=1, tiled=True
    )
    grad = summed / count
    new_first = 0.9 * first_moment + 0.1 * grad
    new_second = 0.95 * second_moment + 0.05 * grad * grad
    bias_first = 1.0 - 0.9**10
    bias_second = 1.0 - 0.95**10
    new_weights = w_spec - 0.01 * (new_first / bias_first) / (
        jnp.sqrt(new_second / bias_second) + 1e-08
    )
    return (layer_out, new_weights, new_first, new_second)


def solution(mesh):
    placed = (
        P("dp", None, "slab", None),
        P("dp", None, "slab", None),
        P("slab", "dp", None, None),
        P("slab", "dp", None, None),
        P("slab", "dp", None, None),
        P(),
        P(),
    )
    return jax.shard_map(
        body,
        mesh=mesh,
        in_specs=placed,
        out_specs=(
            P("dp", None, "slab", None),
            P("slab", "dp", None, None),
            P("slab", "dp", None, None),
            P("slab", "dp", None, None),
        ),
        check_vma=False,
    )
```

profile of v0, /device:TPU:0, one launch (start us, length us, event | category | flops | bytes accessed | tf_op | source)
XLA Modules:
  0.0 820.8 jit_solution(16519467777478254915)
XLA Ops:
  8.2 18.1 %fusion.120 = f32[64,16384]{1,0:T(8,128)S(1)} fusion(bf16[16384,512]{1,0:T(8,128)(2,1)} %bitcast.145, f32[512,32]{0,1:T(8,128)S(1)} %get-tuple-element.19, f32[512,32]{0,1:T(8,128)S(1)} %get-tuple-element.20), kind=kOutput, calls=%fused_computation.154 | convolution fusion | flops 6442483712 | bytes 21102592 | tf_op jit(solution)/shard_map/dot_general | solution.py:69
  35.6 48.7 %all-to-all-done = f32[64,256,2,32]{1,0,2,3:T(8,128)} async-done(((f32[64,256,2,32]{1,0,2,3:T(8,128)}), f32[64,256,2,32]{1,0,2,3:T(8,128)}, u32[]{:S(2)}, u32[]{:S(2)}) %all-to-all-start) | async-done | bytes 4194336 | tf_op jit(solution)/shard_map/all_to_all | solution.py:76
  84.4 7.4 copy.68
  91.8 6.6 reshape.41
  104.5 6.1 fusion.58
  111.6 28.3 %all-gather.2.cloned.1.call-done = f32[16,32,64,128]{3,2,1,0:T(8,128)} async-done(((f32[16,2,64,128]{3,2,1,0:T(8,128)}), f32[16,32,64,128]{3,2,1,0:T(8,128)}) %all-gather.2.cloned.1.call-update) | async-done | bytes 16777232 | tf_op jit(solution)/shard_map/all_gather | solution.py:105
  139.9 17.5 %fusion.121 = f32[16,32,1,128]{3,2,1,0:T(1,128)S(1)} fusion(f32[16,64,32,1]{1,3,2,0:T(1,128)S(1)} %copy.43, f32[16,32,64,128]{3,2,1,0:T(8,128)} %all-gather.2.cloned.1.call-done), kind=kOutput, calls=%fused_computation.156 | convolution fusion | flops 50331648 | bytes 17170432 | tf_op jit(solution)/shard_map/kij,kjio->koj/dot_general | solution.py:109
  157.3 15.1 %fusion.122 = f32[16,32,1,128]{3,2,1,0:T(1,128)S(1)} fusion(f32[16,64,32,1]{1,3,2,0:T(1,128)S(1)} %copy.45, f32[16,32,64,128]{3,2,1,0:T(8,128)S(1)} %copy-done.2), kind=kOutput, calls=%fused_computation.157 | convolution fusion | flops 50331648 | bytes 17170432 | tf_op jit(solution)/shard_map/kij,kjio->koj/dot_general | solution.py:110
  184.1 9.1 %copy.32 = f32[64,512,2,16]{0,3,2,1:T(8,128)} copy(f32[64,512,2,16]{1,0,3,2:T(8,128)} %pad_maximum_fusion.1) | data formatting | bytes 8388608 | tf_op jit(solution)/shard_map/stack | solution.py:87
  193.2 8.7 %reshape.57 = f32[2,1,524288]{2,1,0:T(1,128)} reshape(f32[512,2,16,64]{3,2,1,0:T(8,128)} %bitcast.147) | data formatting | bytes 8388608
  207.8 35.3 %fusion.19 = f32[64,256,512]{2,0,1:T(8,128)} fusion(bf16[64,64]{1,0:T(8,128)(2,1)S(1)} %copy-done, bf16[8,8,256,512]{3,2,1,0:T(8,128)(2,1)} %bitcast.146), kind=kOutput, calls=%fused_computation.21 | convolution fusion | flops 1073741824 | bytes 50339840 | tf_op jit(solution)/shard_map/io,in->on/dot_general | solution.py:115
  243.1 12.5 %all-to-all-done.1 = f32[2,1,524288]{2,1,0:T(1,128)} async-done(((f32[2,1,524288]{2,1,0:T(1,128)}), f32[2,1,524288]{2,1,0:T(1,128)}, u32[]{:S(2)}, u32[]{:S(2)}) %all-to-all-start.1) | async-done | bytes 4194336 | tf_op jit(solution)/shard_map/all_to_all | solution.py:88
  256.1 16.5 %reduce = f32[2,524288]{1,0:T(2,128)} reduce(f32[2,1,524288]{2,1,0:T(1,128)} %all-to-all-done.1, f32[]{:T(128)} %broadcast.184), dimensions={1}, to_apply=%all_to_all.36.reduce_sub_computation | reduce | bytes 8388612 | tf_op jit(solution)/shard_map/all_to_all | solution.py:88
  272.7 10.1 %reshape.58 = f32[512,2,16,64]{3,2,1,0:T(8,128)} reshape(f32[2,524288]{1,0:T(2,128)} %reduce) | data formatting | bytes 8388608
  282.8 8.7 %copy.33 = f32[64,2,256,2,16]{2,4,1,3,0:T(8,128)} copy(f32[64,2,256,2,16]{0,4,3,2,1:T(8,128)} %bitcast.148) | data formatting | bytes 8388608 | tf_op jit(solution)/shard_map/all_to_all | solution.py:88
  291.5 56.3 %fusion.10 = f32[64,256,512]{2,1,0:T(8,128)} fusion(f32[64,256,512]{2,0,1:T(8,128)} %fusion.19, f32[64]{0:T(128)S(1)} %copy-done.6, f32[64,256,64]{1,2,0:T(8,128)} %bitcast.149, f32[32,512]{1,0:T(8,128)S(1)} %get-tuple-element.21, f32[32,512]{1,0:T(8,128)S(1)} %get-tuple-element.22), kind=kOutput, calls=%fused_computation.12 | convolution fusion | flops 6467649536 | bytes 71434496 | tf_op jit(solution)/shard_map/dot_general | solution.py:90
  347.8 57.3 %fusion.7 = f32[64,256,2,32]{1,3,2,0:T(8,128)S(1)} fusion(f32[2,32,512,1]{2,1,0,3:T(8,128)S(1)} %bitcast.162, f32[64,256,512]{2,1,0:T(8,128)} %fusion.10, bf16[1,64,256,512]{3,2,1,0:T(8,128)(2,1)} %param.8), kind=kOutput, calls=%fused_computation.9 | convolution fusion | flops 6601834496 | bytes 54657024 | tf_op jit(solution)/shard_map/dot_general | solution.py:69
  416.4 46.7 %all-to-all-done.2 = f32[64,256,2,32]{1,2,0,3:T(2,128)} async-done(((f32[64,256,2,32]{1,2,0,3:T(2,128)}), f32[64,256,2,32]{1,2,0,3:T(2,128)}, u32[]{:S(2)}, u32[]{:S(2)}) %all-to-all-start.2) | async-done | bytes 4194336 | tf_op jit(solution)/shard_map/all_to_all | solution.py:76
  463.2 7.4 copy.67
  470.6 6.7 reshape.42
  490.4 11.3 %multiply_add_fusion.1 = (f32[16,32,64,64]{3,2,1,0:T(8,128)S(1)}, f32[16,32,64,64]{3,2,1,0:T(8,128)}) fusion(f32[16,32,64]{2,1,0:T(8,128)S(1)} %copy.42, f32[16,32,64]{2,1,0:T(8,128)S(1)} %copy.41, f32[16,32,64]{2,1,0:T(8,128)S(1)} %copy.40, f32[16,32,64]{2,1,0:T(8,128)S(1)} %copy.37), kind=kLoop, calls=%fused_computation.27 | loop fusion | flops 12582912 | bytes 17301504 | tf_op jit(solution)/shard_map/add | solution.py:127
  501.6 13.1 %pad_maximum_fusion = f32[16,32,64,128]{3,2,1,0:T(8,128)} fusion(f32[16,32,64,64]{3,2,1,0:T(8,128)} %get-tuple-element.12, f32[16,32,64,64]{3,2,1,0:T(8,128)S(1)} %get-tuple-element.11), kind=kLoop, calls=%fused_computation.24 | loop fusion | flops 4194304 | bytes 33554432 | tf_op jit(solution)/shard_map/concatenate | solution.py:134
  516.7 22.3 %fusion.28 = bf16[1,64,256,512]{3,2,1,0:T(8,128)(2,1)} fusion(f32[64,256,512]{2,1,0:T(8,128)} %fusion.10), kind=kLoop, calls=%fused_computation.33 | loop fusion | flops 75497472 | bytes 50331648 | tf_op jit(solution)/shard_map/broadcast_in_dim | solution.py:122
  539.0 271.4 %all-reduce.3.cloned.1.call-done = f32[16,32,64,128]{3,2,1,0:T(8,128)} async-done(((f32[16,32,64,128]{3,2,1,0:T(8,128)}), f32[16,32,64,128]{3,2,1,0:T(8,128)}) %all-reduce.3.cloned.1.call-update) | async-done | bytes 16777232
  (55 shorter events, 64.3 us)
Async XLA Ops:
  7.2 200.7 %copy-start = (bf16[64,64]{1,0:T(8,128)(2,1)S(1)}, bf16[64,64]{1,0:T(8,128)(2,1)}, u32[]{:S(2)}) copy-start(bf16[64,64]{1,0:T(8,128)(2,1)} %param.12) | copy-start | bytes 24580
  7.2 132.7 %all-gather.2.cloned.1.call-start = ((), (), s32[]{:S(2)}) async-start(), calls=%async_computation.3 | async-start | bytes 17825792 | tf_op jit(solution)/shard_map/all_gather | solution.py:105
  29.9 54.5 %all-to-all-start = ((f32[64,256,2,32]{1,0,2,3:T(8,128)}), f32[64,256,2,32]{1,0,2,3:T(8,128)}, u32[]{:S(2)}, u32[]{:S(2)}) async-start(f32[64,256,2,32]{1,0,2,3:T(8,128)} %copy.30), calls=%async_computation | async-start | bytes 8388608 | tf_op jit(solution)/shard_map/all_to_all | solution.py:76
  139.9 17.5 %copy-start.2 = (f32[16,32,64,128]{3,2,1,0:T(8,128)S(1)}, f32[16,32,64,128]{3,2,1,0:T(8,128)}, u32[]{:S(2)}) copy-start(f32[16,32,64,128]{3,2,1,0:T(8,128)} %all-gather.2.cloned.1.call-done) | copy-start | bytes 50331652
  201.9 53.7 %all-to-all-start.1 = ((f32[2,1,524288]{2,1,0:T(1,128)}), f32[2,1,524288]{2,1,0:T(1,128)}, u32[]{:S(2)}, u32[]{:S(2)}) async-start(f32[2,1,524288]{2,1,0:T(1,128)} %reshape.57), calls=%async_computation.1 | async-start | bytes 8388608 | tf_op jit(solution)/shard_map/all_to_all | solution.py:88
  256.1 35.4 %copy-start.6 = (f32[64]{0:T(128)S(1)}, f32[64]{0:T(128)}, u32[]{:S(2)}) copy-start(f32[64]{0:T(128)} %param.13) | copy-start | bytes 772
  410.3 52.8 %all-to-all-start.2 = ((f32[64,256,2,32]{1,2,0,3:T(2,128)}), f32[64,256,2,32]{1,2,0,3:T(2,128)}, u32[]{:S(2)}, u32[]{:S(2)}) async-start(f32[64,256,2,32]{1,2,0,3:T(2,128)} %copy.38), calls=%async_computation.2 | async-start | bytes 8388608 | tf_op jit(solution)/shard_map/all_to_all | solution.py:76
  415.9 394.5 %all-reduce.3.cloned.1.call-start = ((), (), s32[]{:S(2)}) async-start(), calls=%async_computation.4 | async-start | bytes 33554432
  514.7 0.7 copy-start.7
  516.0 297.8 %copy-start.1 = (bf16[64,64]{1,0:T(8,128)(2,1)S(1)}, bf16[64,64]{1,0:T(8,128)(2,1)}, u32[]{:S(2)}) copy-start(bf16[64,64]{1,0:T(8,128)(2,1)} %param.12) | copy-start | bytes 24580
  516.6 293.8 %copy-start.3 = (f32[16,2,64,128]{3,2,1,0:T(8,128)S(1)}, f32[16,2,64,128]{3,2,1,0:T(8,128)}, u32[]{:S(2)}) copy-start(f32[16,2,64,128]{3,2,1,0:T(8,128)} %param.9) | copy-start | bytes 3145732
  516.7 293.8 %copy-start.4 = (f32[16,2,64,128]{3,2,1,0:T(8,128)S(1)}, f32[16,2,64,128]{3,2,1,0:T(8,128)}, u32[]{:S(2)}) copy-start(f32[16,2,64,128]{3,2,1,0:T(8,128)} %param.10) | copy-start | bytes 3145732
  516.7 293.8 %copy-start.5 = (f32[16,2,64,128]{3,2,1,0:T(8,128)S(1)}, f32[16,2,64,128]{3,2,1,0:T(8,128)}, u32[]{:S(2)}) copy-start(f32[16,2,64,128]{3,2,1,0:T(8,128)} %param.11) | copy-start | bytes 3145732
Sparse Core Ops, SparseCore 0:
  10.2 129.6 all-gather.1
  514.9 295.4 all-reduce.2
where the time goes:
time: 828 us; the launch traced here: 821 us
  waiting for transfers between devices  408 us (49%)
  matrix products  233 us (28%)
  local copies, waits for them, and re-layouts  77.1 us (9%)
  other arithmetic  70.2 us (8%)
  starting transfers between devices  16.8 us (2%)
  between operations  15.2 us (2%)
    unnamed x3, waiting for transfers between devices  272 us
    all_to_all x2, waiting for transfers between devices, forward_modes(): lax.all_to_all(along_z, 'slab', split_axis=3, concat_axis=1, tiled=True)  95.5 us
    dot_general x2, matrix products, forward_modes(): jnp.dot(field.reshape(chans * rows, length), table, precision=high, prefe...  75.4 us
    dot_general x1, matrix products, inverse_modes(): jnp.dot(slabs.reshape(chans * rows, 2 * KZ), back_table, precision=high,...  56.3 us
    dot_general x1, matrix products, body(): jnp.einsum('io,in->on', w_skip, field_low.reshape(chans, rows * length),...  35.3 us
    all_gather x1, waiting for transfers between devices, body(): weights = lax.all_gather(w_spec, 'dp', axis=1, tiled=True)  28.3 us
    broadcast_in_dim x1, other arithmetic, body(): layer_out = gelu_value(pre).astype(jnp.bfloat16)[None]  22.3 us
    unnamed x20, local copies, waits for them, and re-layouts  21.4 us
  transfers between devices with their start and end apart: 5, of which 5 were waited for; matrix products, arithmetic and copies ran while one was open for 13% of the time, Pallas kernels for 0%

commit v1 on v0

--- a/solution.py
+++ b/solution.py
@@ -102,7 +102,24 @@
     out_scale = 1.0 / math.sqrt(KY * KZ)
     count = lax.axis_size("dp")
     field_low = snapshots[0]
-    weights = lax.all_gather(w_spec, "dp", axis=1, tiled=True)
+    count_2, index, extent = (lax.axis_size("dp"), lax.axis_index("dp"), w_spec.shape[1])
+    right = [(i, (i + 1) % count_2) for i in range(count_2)]
+    left = [(i, (i - 1) % count_2) for i in range(count_2)]
+    filled = jnp.zeros((*w_spec.shape[:1], count_2 * extent, *w_spec.shape[1 + 1 :]), w_spec.dtype)
+    filled = lax.dynamic_update_slice_in_dim(filled, w_spec, index * extent, axis=1)
+    from_left = from_right = w_spec
+    middle = count_2 // 2
+    for hop in range(1, middle + 1):
+        from_left = lax.ppermute(from_left, "dp", right)
+        filled = lax.dynamic_update_slice_in_dim(
+            filled, from_left, (index - hop) % count_2 * extent, axis=1
+        )
+        if hop < count_2 - middle:
+            from_right = lax.ppermute(from_right, "dp", left)
+            filled = lax.dynamic_update_slice_in_dim(
+                filled, from_right, (index + hop) % count_2 * extent, axis=1
+            )
+    weights = filled
     spec_u = forward_modes(field_low.astype(jnp.float32)) * spec_scale
     ureal = spec_u[:, 0]
     uimag = spec_u[:, 1]

time: 828 us -> 929 us (1.12)
  starting transfers between devices: 16.8 us -> 118 us
  waiting for transfers between devices: 408 us -> 369 us
  local copies, waits for them, and re-layouts: 77.1 us -> 114 us
    ppermute x0 -> x15, starting transfers between devices: none -> 101 us  [the longest x8 86.1 us: body(): from_left = lax.ppermute(from_left, 'dp', right)]
    all_to_all x2, waiting for transfers between devices: 95.5 us -> 56.4 us  [forward_modes(): lax.all_to_all(along_z, 'slab', split_axis=3, concat_axis=1, tiled=True)]
    ppermute x0 -> x15, waiting for transfers between devices: none -> 29.1 us  [the longest x8 25 us: body(): from_left = lax.ppermute(from_left, 'dp', right)]
    all_gather x1 -> x0, waiting for transfers between devices: 28.3 us -> none  [body(): weights = lax.all_gather(w_spec, 'dp', axis=1, tiled=True)]
    dynamic_update_slice x0 -> x16, local copies, waits for them, and re-layouts: none -> 28.1 us  [the longest x7 13.6 us: body(): lax.dynamic_update_slice_in_dim(filled, from_right, (index + hop) % count...]
    unnamed x3 -> x2, waiting for transfers between devices: 272 us -> 272 us
    unnamed x20 -> x36, local copies, waits for them, and re-layouts: 21.4 us -> 21.4 us
  transfers between devices with their start and end apart: 5 -> 19, of which waited for: 5 -> 9; matrix products, arithmetic and copies ran while one was open for 13% -> 16% of each run, Pallas kernels for 0% -> 0%
where the time goes in v1:
time: 929 us; the launch traced here: 922 us
  waiting for transfers between devices  369 us (40%)
  matrix products  235 us (25%)
  starting transfers between devices  118 us (13%)
  local copies, waits for them, and re-layouts  114 us (12%)
  other arithmetic  70.2 us (8%)
  between operations  15.5 us (2%)
    unnamed x2, waiting for transfers between devices  272 us
    ppermute x8, starting transfers between devices, body(): from_left = lax.ppermute(from_left, 'dp', right)  86.1 us
    dot_general x2, matrix products, forward_modes(): jnp.dot(field.reshape(chans * rows, length), table, precision=high, prefe...  75.4 us
    all_to_all x2, waiting for transfers between devices, forward_modes(): lax.all_to_all(along_z, 'slab', split_axis=3, concat_axis=1, tiled=True)  56.4 us
    dot_general x1, matrix products, inverse_modes(): jnp.dot(slabs.reshape(chans * rows, 2 * KZ), back_table, precision=high,...  56.1 us
    dot_general x1, matrix products, body(): jnp.einsum('io,in->on', w_skip, field_low.reshape(chans, rows * length),...  35.5 us
    ppermute x8, waiting for transfers between devices, body(): from_left = lax.ppermute(from_left, 'dp', right)  25 us
    broadcast_in_dim x1, other arithmetic, body(): layer_out = gelu_value(pre).astype(jnp.bfloat16)[None]  22.2 us
  transfers between devices with their start and end apart: 19, of which 9 were waited for; matrix products, arithmetic and copies ran while one was open for 16% of the time, Pallas kernels for 0%

profile of v1, /device:TPU:0, one launch (start us, length us, event | category | flops | bytes accessed | tf_op | source)
XLA Modules:
  0.0 921.6 jit_solution(17835753755988802782)
XLA Ops:
  12.7 12.7 %collective-permute-done = f32[16,2,64,128]{3,2,1,0:T(8,128)S(1)} collective-permute-done((f32[16,2,64,128]{3,2,1,0:T(8,128)}, f32[16,2,64,128]{3,2,1,0:T(8,128)S(1)}, u32[]{:S(2)}, u32[]{:S(2)}) %collective-permute-start) | collective-permute-done | bytes 1048608 | tf_op jit(solution)/shard_map/ppermute | solution.py:113
  33.6 8.9 collective-permute-done.2
  42.5 15.8 %collective-permute-start.4 = (f32[16,2,64,128]{3,2,1,0:T(8,128)S(1)}, f32[16,2,64,128]{3,2,1,0:T(8,128)}, u32[]{:S(2)}, u32[]{:S(2)}) collective-permute-start(f32[16,2,64,128]{3,2,1,0:T(8,128)S(1)} %collective-permute-done.2), channel_id=1, source_target_pairs={{0,2},{2,4},{4,6},{6,8},{8,10},{10,12},{12,14},{14,16},{16,18},{18... | collective-permute-start | bytes 3145736 | tf_op jit(solution)/shard_map/ppermute | solution.py:113
  62.0 21.6 %collective-permute-start.6 = (f32[16,2,64,128]{3,2,1,0:T(8,128)}, f32[16,2,64,128]{3,2,1,0:T(8,128)S(1)}, u32[]{:S(2)}, u32[]{:S(2)}) collective-permute-start(f32[16,2,64,128]{3,2,1,0:T(8,128)} %collective-permute-done.4), channel_id=1, source_target_pairs={{0,2},{2,4},{4,6},{6,8},{8,10},{10,12},{12,14},{14,16},{16,18},{18... | collective-permute-start | bytes 3145736 | tf_op jit(solution)/shard_map/ppermute | solution.py:113
  83.6 18.1 %fusion.120 = f32[64,16384]{1,0:T(8,128)S(1)} fusion(bf16[16384,512]{1,0:T(8,128)(2,1)} %bitcast.145, f32[512,32]{0,1:T(8,128)S(1)} %get-tuple-element.19, f32[512,32]{0,1:T(8,128)S(1)} %get-tuple-element.20), kind=kOutput, calls=%fused_computation.170 | convolution fusion | flops 6442483712 | bytes 21102592 | tf_op jit(solution)/shard_map/dot_general | solution.py:69
  128.3 19.0 %collective-permute-start.10 = (f32[16,2,64,128]{3,2,1,0:T(8,128)}, f32[16,2,64,128]{3,2,1,0:T(8,128)}, u32[]{:S(2)}, u32[]{:S(2)}) collective-permute-start(f32[16,2,64,128]{3,2,1,0:T(8,128)} %collective-permute-done.8), channel_id=1, source_target_pairs={{0,2},{2,4},{4,6},{6,8},{8,10},{10,12},{12,14},{14,16},{16,18},{18... | collective-permute-start | bytes 3145736 | tf_op jit(solution)/shard_map/ppermute | solution.py:113
  149.5 8.5 all-to-all-done
  204.0 17.0 %collective-permute-start.14 = (f32[16,2,64,128]{3,2,1,0:T(8,128)}, f32[16,2,64,128]{3,2,1,0:T(8,128)S(1)}, u32[]{:S(2)}, u32[]{:S(2)}) collective-permute-start(f32[16,2,64,128]{3,2,1,0:T(8,128)} %collective-permute-done.12), channel_id=1, source_target_pairs={{0,2},{2,4},{4,6},{6,8},{8,10},{10,12},{12,14},{14,16},{16,18},{18... | collective-permute-start | bytes 3145736 | tf_op jit(solution)/shard_map/ppermute | solution.py:113
  237.9 16.8 %fusion.122 = f32[16,32,1,128]{3,2,1,0:T(1,128)S(1)} fusion(f32[16,32,64,128]{3,2,1,0:T(8,128)} %constant_dynamic-update-slice_fusion, f32[16,64,32,1]{1,3,2,0:T(1,128)S(1)} %copy.45), kind=kOutput, calls=%fused_computation.173 | convolution fusion | flops 50331648 | bytes 17170432 | tf_op jit(solution)/shard_map/kij,kjio->koj/dot_general | solution.py:127
  254.8 17.0 %fusion.121 = f32[16,32,1,128]{3,2,1,0:T(1,128)S(1)} fusion(f32[16,32,64,128]{3,2,1,0:T(8,128)} %constant_dynamic-update-slice_fusion, f32[16,64,32,1]{1,3,2,0:T(1,128)S(1)} %copy.43), kind=kOutput, calls=%fused_computation.172 | convolution fusion | flops 50331648 | bytes 17170432 | tf_op jit(solution)/shard_map/kij,kjio->koj/dot_general | solution.py:126
  283.6 9.1 copy.32
  292.7 8.8 reshape.57
  307.4 35.5 %fusion.19 = f32[64,256,512]{2,0,1:T(8,128)} fusion(bf16[64,64]{1,0:T(8,128)(2,1)S(1)} %copy-done, bf16[8,8,256,512]{3,2,1,0:T(8,128)(2,1)} %bitcast.146), kind=kOutput, calls=%fused_computation.21 | convolution fusion | flops 1073741824 | bytes 50339840 | tf_op jit(solution)/shard_map/io,in->on/dot_general | solution.py:132
  342.9 11.4 %all-to-all-done.1 = f32[2,1,524288]{2,1,0:T(1,128)} async-done(((f32[2,1,524288]{2,1,0:T(1,128)}), f32[2,1,524288]{2,1,0:T(1,128)}, u32[]{:S(2)}, u32[]{:S(2)}) %all-to-all-start.1) | async-done | bytes 4194336 | tf_op jit(solution)/shard_map/all_to_all | solution.py:88
  354.8 16.6 %reduce = f32[2,524288]{1,0:T(2,128)} reduce(f32[2,1,524288]{2,1,0:T(1,128)} %all-to-all-done.1, f32[]{:T(128)} %broadcast.199), dimensions={1}, to_apply=%all_to_all.36.reduce_sub_computation | reduce | bytes 8388612 | tf_op jit(solution)/shard_map/all_to_all | solution.py:88
  371.4 10.1 %reshape.58 = f32[512,2,16,64]{3,2,1,0:T(8,128)} reshape(f32[2,524288]{1,0:T(2,128)} %reduce) | data formatting | bytes 8388608
  381.5 8.7 copy.33
  390.2 56.1 %fusion.10 = f32[64,256,512]{2,1,0:T(8,128)} fusion(f32[64,256,512]{2,0,1:T(8,128)} %fusion.19, f32[64]{0:T(128)S(1)} %copy-done.14, f32[64,256,64]{1,2,0:T(8,128)} %bitcast.149, f32[32,512]{1,0:T(8,128)S(1)} %get-tuple-element.21, f32[32,512]{1,0:T(8,128)S(1)} %get-tuple-element.22), kind=kOutput, calls=%fused_computation.12 | convolution fusion | flops 6467649536 | bytes 71434496 | tf_op jit(solution)/shard_map/dot_general | solution.py:90
  446.3 57.3 %fusion.7 = f32[64,256,2,32]{1,3,2,0:T(8,128)S(1)} fusion(f32[2,32,512,1]{2,1,0,3:T(8,128)S(1)} %bitcast.162, f32[64,256,512]{2,1,0:T(8,128)} %fusion.10, bf16[1,64,256,512]{3,2,1,0:T(8,128)(2,1)} %param.8), kind=kOutput, calls=%fused_computation.9 | convolution fusion | flops 6601834496 | bytes 54657024 | tf_op jit(solution)/shard_map/dot_general | solution.py:69
  515.0 47.9 %all-to-all-done.2 = f32[64,256,2,32]{1,2,0,3:T(2,128)} async-done(((f32[64,256,2,32]{1,2,0,3:T(2,128)}), f32[64,256,2,32]{1,2,0,3:T(2,128)}, u32[]{:S(2)}, u32[]{:S(2)}) %all-to-all-start.2) | async-done | bytes 4194336 | tf_op jit(solution)/shard_map/all_to_all | solution.py:76
  590.1 11.3 %multiply_add_fusion.1 = (f32[16,32,64,64]{3,2,1,0:T(8,128)S(1)}, f32[16,32,64,64]{3,2,1,0:T(8,128)}) fusion(f32[16,32,64]{2,1,0:T(8,128)S(1)} %copy.42, f32[16,32,64]{2,1,0:T(8,128)S(1)} %copy.41, f32[16,32,64]{2,1,0:T(8,128)S(1)} %copy.40, f32[16,32,64]{2,1,0:T(8,128)S(1)} %copy.37), kind=kLoop, calls=%fused_computation.27 | loop fusion | flops 12582912 | bytes 17301504 | tf_op jit(solution)/shard_map/add | solution.py:144
  601.3 13.1 %pad_maximum_fusion = f32[16,32,64,128]{3,2,1,0:T(8,128)} fusion(f32[16,32,64,64]{3,2,1,0:T(8,128)} %get-tuple-element.12, f32[16,32,64,64]{3,2,1,0:T(8,128)S(1)} %get-tuple-element.11), kind=kLoop, calls=%fused_computation.24 | loop fusion | flops 4194304 | bytes 33554432 | tf_op jit(solution)/shard_map/concatenate | solution.py:151
  616.4 22.2 %fusion.28 = bf16[1,64,256,512]{3,2,1,0:T(8,128)(2,1)} fusion(f32[64,256,512]{2,1,0:T(8,128)} %fusion.10), kind=kLoop, calls=%fused_computation.33 | loop fusion | flops 75497472 | bytes 50331648 | tf_op jit(solution)/shard_map/broadcast_in_dim | solution.py:139
  638.6 272.3 %all-reduce.3.cloned.1.call-done = f32[16,32,64,128]{3,2,1,0:T(8,128)} async-done(((f32[16,32,64,128]{3,2,1,0:T(8,128)}), f32[16,32,64,128]{3,2,1,0:T(8,128)}) %all-reduce.3.cloned.1.call-update) | async-done | bytes 16777232
  (115 shorter events, 170.3 us)
Async XLA Ops:
  7.2 300.2 %copy-start = (bf16[64,64]{1,0:T(8,128)(2,1)S(1)}, bf16[64,64]{1,0:T(8,128)(2,1)}, u32[]{:S(2)}) copy-start(bf16[64,64]{1,0:T(8,128)(2,1)} %param.12) | copy-start | bytes 24580
  7.2 18.3 %collective-permute-start = (f32[16,2,64,128]{3,2,1,0:T(8,128)}, f32[16,2,64,128]{3,2,1,0:T(8,128)S(1)}, u32[]{:S(2)}, u32[]{:S(2)}) collective-permute-start(f32[16,2,64,128]{3,2,1,0:T(8,128)} %param.9), channel_id=1, source_target_pairs={{0,2},{2,4},{4,6},{6,8},{8,10},{10,12},{12,14},{14,16},{16,18},{18... | collective-permute-start | bytes 3145736 | tf_op jit(solution)/shard_map/ppermute | solution.py:113
  7.7 25.9 %collective-permute-start.1 = (f32[16,2,64,128]{3,2,1,0:T(8,128)}, f32[16,2,64,128]{3,2,1,0:T(8,128)S(1)}, u32[]{:S(2)}, u32[]{:S(2)}) collective-permute-start(f32[16,2,64,128]{3,2,1,0:T(8,128)} %param.9), channel_id=1, source_target_pairs={{0,30},{2,0},{4,2},{6,4},{8,6},{10,8},{12,10},{14,12},{16,14},{18,... | collective-permute-start | bytes 3145736 | tf_op jit(solution)/shard_map/ppermute | solution.py:118
  25.5 17.0 %collective-permute-start.2 = (f32[16,2,64,128]{3,2,1,0:T(8,128)S(1)}, f32[16,2,64,128]{3,2,1,0:T(8,128)S(1)}, u32[]{:S(2)}, u32[]{:S(2)}) collective-permute-start(f32[16,2,64,128]{3,2,1,0:T(8,128)S(1)} %collective-permute-done), channel_id=1, source_target_pairs={{0,2},{2,4},{4,6},{6,8},{8,10},{10,12},{12,14},{14,16},{16,18},{18... | collective-permute-start | bytes 3145736 | tf_op jit(solution)/shard_map/ppermute | solution.py:113
  33.6 25.0 %collective-permute-start.3 = (f32[16,2,64,128]{3,2,1,0:T(8,128)S(1)}, f32[16,2,64,128]{3,2,1,0:T(8,128)}, u32[]{:S(2)}, u32[]{:S(2)}) collective-permute-start(f32[16,2,64,128]{3,2,1,0:T(8,128)S(1)} %collective-permute-done.1), channel_id=1, source_target_pairs={{0,30},{2,0},{4,2},{6,4},{8,6},{10,8},{12,10},{14,12},{16,14},{18,... | collective-permute-start | bytes 3145736 | tf_op jit(solution)/shard_map/ppermute | solution.py:118
  42.5 19.5 %collective-permute-start.4 = (f32[16,2,64,128]{3,2,1,0:T(8,128)S(1)}, f32[16,2,64,128]{3,2,1,0:T(8,128)}, u32[]{:S(2)}, u32[]{:S(2)}) collective-permute-start(f32[16,2,64,128]{3,2,1,0:T(8,128)S(1)} %collective-permute-done.2), channel_id=1, source_target_pairs={{0,2},{2,4},{4,6},{6,8},{8,10},{10,12},{12,14},{14,16},{16,18},{18... | collective-permute-start | bytes 3145736 | tf_op jit(solution)/shard_map/ppermute | solution.py:113
  58.6 52.3 %collective-permute-start.5 = (f32[16,2,64,128]{3,2,1,0:T(8,128)}, f32[16,2,64,128]{3,2,1,0:T(8,128)}, u32[]{:S(2)}, u32[]{:S(2)}) collective-permute-start(f32[16,2,64,128]{3,2,1,0:T(8,128)} %collective-permute-done.3), channel_id=1, source_target_pairs={{0,30},{2,0},{4,2},{6,4},{8,6},{10,8},{12,10},{14,12},{16,14},{18,... | collective-permute-start | bytes 3145736 | tf_op jit(solution)/shard_map/ppermute | solution.py:118
  62.0 49.0 %collective-permute-start.6 = (f32[16,2,64,128]{3,2,1,0:T(8,128)}, f32[16,2,64,128]{3,2,1,0:T(8,128)S(1)}, u32[]{:S(2)}, u32[]{:S(2)}) collective-permute-start(f32[16,2,64,128]{3,2,1,0:T(8,128)} %collective-permute-done.4), channel_id=1, source_target_pairs={{0,2},{2,4},{4,6},{6,8},{8,10},{10,12},{12,14},{14,16},{16,18},{18... | collective-permute-start | bytes 3145736 | tf_op jit(solution)/shard_map/ppermute | solution.py:113
  105.3 52.7 %all-to-all-start = ((f32[64,256,2,32]{1,0,2,3:T(8,128)}), f32[64,256,2,32]{1,0,2,3:T(8,128)}, u32[]{:S(2)}, u32[]{:S(2)}) async-start(f32[64,256,2,32]{1,0,2,3:T(8,128)} %copy.30), calls=%async_computation | async-start | bytes 8388608 | tf_op jit(solution)/shard_map/all_to_all | solution.py:76
  110.9 12.7 %collective-permute-start.7 = (f32[16,2,64,128]{3,2,1,0:T(8,128)}, f32[16,2,64,128]{3,2,1,0:T(8,128)}, u32[]{:S(2)}, u32[]{:S(2)}) collective-permute-start(f32[16,2,64,128]{3,2,1,0:T(8,128)} %collective-permute-done.5), channel_id=1, source_target_pairs={{0,30},{2,0},{4,2},{6,4},{8,6},{10,8},{12,10},{14,12},{16,14},{18,... | collective-permute-start | bytes 3145736 | tf_op jit(solution)/shard_map/ppermute | solution.py:118
  111.0 17.3 %collective-permute-start.8 = (f32[16,2,64,128]{3,2,1,0:T(8,128)S(1)}, f32[16,2,64,128]{3,2,1,0:T(8,128)}, u32[]{:S(2)}, u32[]{:S(2)}) collective-permute-start(f32[16,2,64,128]{3,2,1,0:T(8,128)S(1)} %collective-permute-done.6), channel_id=1, source_target_pairs={{0,2},{2,4},{4,6},{6,8},{8,10},{10,12},{12,14},{14,16},{16,18},{18... | collective-permute-start | bytes 3145736 | tf_op jit(solution)/shard_map/ppermute | solution.py:113
  123.6 60.6 %collective-permute-start.9 = (f32[16,2,64,128]{3,2,1,0:T(8,128)}, f32[16,2,64,128]{3,2,1,0:T(8,128)}, u32[]{:S(2)}, u32[]{:S(2)}) collective-permute-start(f32[16,2,64,128]{3,2,1,0:T(8,128)} %collective-permute-done.7), channel_id=1, source_target_pairs={{0,30},{2,0},{4,2},{6,4},{8,6},{10,8},{12,10},{14,12},{16,14},{18,... | collective-permute-start | bytes 3145736 | tf_op jit(solution)/shard_map/ppermute | solution.py:118
  128.3 56.0 %collective-permute-start.10 = (f32[16,2,64,128]{3,2,1,0:T(8,128)}, f32[16,2,64,128]{3,2,1,0:T(8,128)}, u32[]{:S(2)}, u32[]{:S(2)}) collective-permute-start(f32[16,2,64,128]{3,2,1,0:T(8,128)} %collective-permute-done.8), channel_id=1, source_target_pairs={{0,2},{2,4},{4,6},{6,8},{8,10},{10,12},{12,14},{14,16},{16,18},{18... | collective-permute-start | bytes 3145736 | tf_op jit(solution)/shard_map/ppermute | solution.py:113
  184.2 12.7 %collective-permute-start.11 = (f32[16,2,64,128]{3,2,1,0:T(8,128)}, f32[16,2,64,128]{3,2,1,0:T(8,128)}, u32[]{:S(2)}, u32[]{:S(2)}) collective-permute-start(f32[16,2,64,128]{3,2,1,0:T(8,128)} %collective-permute-done.9), channel_id=1, source_target_pairs={{0,30},{2,0},{4,2},{6,4},{8,6},{10,8},{12,10},{14,12},{16,14},{18,... | collective-permute-start | bytes 3145736 | tf_op jit(solution)/shard_map/ppermute | solution.py:118
  184.3 19.6 %collective-permute-start.12 = (f32[16,2,64,128]{3,2,1,0:T(8,128)}, f32[16,2,64,128]{3,2,1,0:T(8,128)}, u32[]{:S(2)}, u32[]{:S(2)}) collective-permute-start(f32[16,2,64,128]{3,2,1,0:T(8,128)} %collective-permute-done.10), channel_id=1, source_target_pairs={{0,2},{2,4},{4,6},{6,8},{8,10},{10,12},{12,14},{14,16},{16,18},{18... | collective-permute-start | bytes 3145736 | tf_op jit(solution)/shard_map/ppermute | solution.py:113
  196.9 38.9 %collective-permute-start.13 = (f32[16,2,64,128]{3,2,1,0:T(8,128)}, f32[16,2,64,128]{3,2,1,0:T(8,128)S(1)}, u32[]{:S(2)}, u32[]{:S(2)}) collective-permute-start(f32[16,2,64,128]{3,2,1,0:T(8,128)} %collective-permute-done.11), channel_id=1, source_target_pairs={{0,30},{2,0},{4,2},{6,4},{8,6},{10,8},{12,10},{14,12},{16,14},{18,... | collective-permute-start | bytes 3145736 | tf_op jit(solution)/shard_map/ppermute | solution.py:118
  204.0 32.9 %collective-permute-start.14 = (f32[16,2,64,128]{3,2,1,0:T(8,128)}, f32[16,2,64,128]{3,2,1,0:T(8,128)S(1)}, u32[]{:S(2)}, u32[]{:S(2)}) collective-permute-start(f32[16,2,64,128]{3,2,1,0:T(8,128)} %collective-permute-done.12), channel_id=1, source_target_pairs={{0,2},{2,4},{4,6},{6,8},{8,10},{10,12},{12,14},{14,16},{16,18},{18... | collective-permute-start | bytes 3145736 | tf_op jit(solution)/shard_map/ppermute | solution.py:113
  301.5 52.9 %all-to-all-start.1 = ((f32[2,1,524288]{2,1,0:T(1,128)}), f32[2,1,524288]{2,1,0:T(1,128)}, u32[]{:S(2)}, u32[]{:S(2)}) async-start(f32[2,1,524288]{2,1,0:T(1,128)} %reshape.57), calls=%async_computation.1 | async-start | bytes 8388608 | tf_op jit(solution)/shard_map/all_to_all | solution.py:88
  508.8 54.1 %all-to-all-start.2 = ((f32[64,256,2,32]{1,2,0,3:T(2,128)}), f32[64,256,2,32]{1,2,0,3:T(2,128)}, u32[]{:S(2)}, u32[]{:S(2)}) async-start(f32[64,256,2,32]{1,2,0,3:T(2,128)} %copy.38), calls=%async_computation.2 | async-start | bytes 8388608 | tf_op jit(solution)/shard_map/all_to_all | solution.py:76
  514.4 396.5 %all-reduce.3.cloned.1.call-start = ((), (), s32[]{:S(2)}) async-start(), calls=%async_computation.3 | async-start | bytes 33554432
  615.7 298.6 %copy-start.1 = (bf16[64,64]{1,0:T(8,128)(2,1)S(1)}, bf16[64,64]{1,0:T(8,128)(2,1)}, u32[]{:S(2)}) copy-start(bf16[64,64]{1,0:T(8,128)(2,1)} %param.12) | copy-start | bytes 24580
  616.4 294.5 %copy-start.3 = (f32[16,2,64,128]{3,2,1,0:T(8,128)S(1)}, f32[16,2,64,128]{3,2,1,0:T(8,128)}, u32[]{:S(2)}) copy-start(f32[16,2,64,128]{3,2,1,0:T(8,128)} %param.9) | copy-start | bytes 3145732
  616.4 294.5 %copy-start.10 = (f32[16,2,64,128]{3,2,1,0:T(8,128)S(1)}, f32[16,2,64,128]{3,2,1,0:T(8,128)}, u32[]{:S(2)}) copy-start(f32[16,2,64,128]{3,2,1,0:T(8,128)} %param.10) | copy-start | bytes 3145732
  616.4 294.5 %copy-start.11 = (f32[16,2,64,128]{3,2,1,0:T(8,128)S(1)}, f32[16,2,64,128]{3,2,1,0:T(8,128)}, u32[]{:S(2)}) copy-start(f32[16,2,64,128]{3,2,1,0:T(8,128)} %param.11) | copy-start | bytes 3145732
  (11 other events, 268.3 us)
Sparse Core Ops, SparseCore 0:
  614.6 296.2 all-reduce.2
